TPU v7x, 32 devices: a whole 2x2x4 slice. The times are simulated.
32 devices in a mesh: dp: 16 (over z, x, core), group: 2 (over y).
Axes of the slice: x: 2, y: 2, z: 4, core: 2. Of those that a mesh axis runs over, the one named last changes fastest.
Arguments:
- tokens: bfloat16 [8192, 896], P(('dp', 'group')), may hold values from -6 to 6
- cotangent: bfloat16 [8192, 896], P(('dp', 'group')), may hold values from -6 to 6
- lengths: int32 [32, 4], P(('dp', 'group')), may hold values from 0 to 256, as said below
- qkv_weight: float32 [896, 1152], P('group'), may hold values from -0.1875 to 0.1875
- out_weight: float32 [896, 896], P('group'), may hold values from -2 to 2
- expand_weight: float32 [896, 9728], P('group'), may hold values from -0.1875 to 0.1875
- down_weight: float32 [4864, 896], P('group'), may hold values from -0.15625 to 0.15625
- norm_gains: float32 [1792], P('group'), may hold values from 0.5 to 1.5
- qkv_biases: float32 [1152], P('group'), may hold values from -1.5 to 1.5
- qkv_first: float32 [896, 1152], P('group'), may hold values from -80 to 80
- out_first: float32 [896, 896], P('group'), may hold values from -10 to 10
- expand_first: float32 [896, 9728], P('group'), may hold values from -24 to 24
- down_first: float32 [4864, 896], P('group'), may hold values from -32 to 32
- gains_first: float32 [1792], P('group'), may hold values from -80 to 80
- biases_first: float32 [1152], P('group'), may hold values from -80 to 80
- qkv_second: float32 [896, 1152], P('group'), may hold values from 18.432 to 73.728
- out_second: float32 [896, 896], P('group'), may hold values from 0.18432 to 0.73728
- expand_second: float32 [896, 9728], P('group'), may hold values from 1.31072 to 5.24288
- down_second: float32 [4864, 896], P('group'), may hold values from 2.94912 to 11.79648
- gains_second: float32 [1792], P('group'), may hold values from 18.432 to 73.728
- biases_second: float32 [1152], P('group'), may hold values from 18.432 to 73.728
Outputs:
- output: bfloat16 [8192, 896], P(('dp', 'group'))
- token_grad: bfloat16 [8192, 896], P(('dp', 'group'))
- qkv_gradient: bfloat16 [896, 1152], P('group')
- out_gradient: bfloat16 [896, 896], P('group')
- expand_gradient: bfloat16 [896, 9728], P('group')
- down_gradient: bfloat16 [4864, 896], P('group')
- gains_gradient: bfloat16 [1792], P('group')
- biases_gradient: bfloat16 [1152], P('group')
- qkv_updated: float32 [896, 1152], P('group')
- out_updated: float32 [896, 896], P('group')
- expand_updated: float32 [896, 9728], P('group')
- down_updated: float32 [4864, 896], P('group')
- gains_updated: float32 [1792], P('group')
- biases_updated: float32 [1152], P('group')
- qkv_momentum: float32 [896, 1152], P('group')
- out_momentum: float32 [896, 896], P('group')
- expand_momentum: float32 [896, 9728], P('group')
- down_momentum: float32 [4864, 896], P('group')
- gains_momentum: float32 [1792], P('group')
- biases_momentum: float32 [1152], P('group')
- qkv_variance: float32 [896, 1152], P('group')
- out_variance: float32 [896, 896], P('group')
- expand_variance: float32 [896, 9728], P('group')
- down_variance: float32 [4864, 896], P('group')
- gains_variance: float32 [1792], P('group')
- biases_variance: float32 [1152], P('group')
Inputs may be any that keep to these rules, and one draw needn't show every extreme that they name: Row r lists the lengths of the sequences packed from the first of device r's 256 rows; a row's lengths sum to 128 or more and to 256 at most, and a length may be 0; in every draw one device holds a single sequence of 256 rows.
All inputs are finite; a program needn't handle non-finite values.
Results may differ from a plain program's by a relative error of at most 0.014.
The roundings to bfloat16 on the way count: a program that leaves them out, or rounds other values in their place, can miss the bound.
Values may be sent and summed in bfloat16 or wider, within the bound.
A program may use at most 512 MiB of HBM per device.

v0:
```python
import jax
import jax.numpy as jnp
from jax import lax
from jax.sharding import PartitionSpec as P

D = 896
HEADS = 14
KV_HEADS = 2
HEAD_DIM = 64
STEP = 10


EPS_NORM = 1e-06
THETA = 1000000.0
MASKED = -1e30
BETA_ONE = 0.9
BETA_TWO = 0.999
EPS_ADAM = 1e-08
DECAY = 0.1
RATE_MATRIX = 0.08
RATE_OUT = 0.8
RATE_VECTOR = 0.6


def layout(length_row, row_count):
    seq_ends = jnp.cumsum(length_row)
    row_ids = jnp.arange(row_count, dtype=jnp.int32)
    segment = jnp.sum((row_ids[:, None] >= seq_ends[None, :]).astype(jnp.int32), axis=1)
    seq_starts = jnp.concatenate([jnp.zeros((1,), jnp.int32), seq_ends])
    slot_ids = jnp.arange(seq_starts.shape[0], dtype=jnp.int32)
    seq_begin = jnp.sum(
        jnp.where(segment[:, None] == slot_ids[None, :], seq_starts[None, :], 0), axis=1
    )
    return (segment, row_ids - seq_begin, row_ids < seq_ends[-1])


def rope_tables(position, head_size):
    half_dim = head_size // 2
    frequency = THETA ** (-(jnp.arange(half_dim, dtype=jnp.float32) * (2.0 / head_size)))
    angles = position.astype(jnp.float32)[:, None] * frequency[None, :]
    return (jnp.cos(angles), jnp.sin(angles))


def rotate(values, cosine, sine_table):
    half_dim = values.shape[-1] // 2
    first_half = values[..., :half_dim]
    second_half = values[..., half_dim:]
    cos_b = cosine[:, None, :]
    sin_b = sine_table[:, None, :]
    return jnp.concatenate(
        [first_half * cos_b - second_half * sin_b, second_half * cos_b + first_half * sin_b],
        axis=-1,
    )


def normalize(values, gain_row):
    scaling = lax.rsqrt(jnp.mean(values * values, axis=-1, keepdims=True) + EPS_NORM)
    return values * scaling * gain_row


def swiglu(expanded):
    half_cols = expanded.shape[1] // 2
    return jax.nn.silu(expanded[:, :half_cols]) * expanded[:, half_cols:]


def adamw(master, first_old, second_old, gradient, step_rate, decay_rate):
    first_new = BETA_ONE * first_old + (1.0 - BETA_ONE) * gradient
    second_new = BETA_TWO * second_old + (1.0 - BETA_TWO) * gradient * gradient
    direction = (
        first_new
        / (1.0 - BETA_ONE**STEP)
        / (jnp.sqrt(second_new / (1.0 - BETA_TWO**STEP)) + EPS_ADAM)
    )
    return (master - step_rate * (direction + decay_rate * master), first_new, second_new)


def local(
    tokens,
    cotangent,
    lengths,
    qkv_weight,
    out_weight,
    expand_weight,
    down_weight,
    norm_gains,
    qkv_biases,
    qkv_first,
    out_first,
    expand_first,
    down_first,
    gains_first,
    biases_first,
    qkv_second,
    out_second,
    expand_second,
    down_second,
    gains_second,
    biases_second,
):
    masters = (qkv_weight, out_weight, expand_weight, down_weight, norm_gains, qkv_biases)
    firsts = (qkv_first, out_first, expand_first, down_first, gains_first, biases_first)
    seconds = (qkv_second, out_second, expand_second, down_second, gains_second, biases_second)
    w_qkv, w_out, w_expand, w_down, gains_low, biases_low = (
        lax.all_gather(qkv_weight.astype(jnp.bfloat16), "group", axis=0, tiled=True),
        lax.all_gather(out_weight.astype(jnp.bfloat16), "group", axis=0, tiled=True),
        lax.all_gather(expand_weight.astype(jnp.bfloat16), "group", axis=0, tiled=True),
        lax.all_gather(down_weight.astype(jnp.bfloat16), "group", axis=0, tiled=True),
        lax.all_gather(norm_gains.astype(jnp.bfloat16), "group", axis=0, tiled=True),
        lax.all_gather(qkv_biases.astype(jnp.bfloat16), "group", axis=0, tiled=True),
    )
    row_count = tokens.shape[0]
    block_rows = min(512, row_count)
    kv_width = KV_HEADS * HEAD_DIM
    repeat = HEADS // KV_HEADS
    scaling = HEAD_DIM ** (-0.5)
    segment, position, valid_flag = layout(lengths[0], row_count)
    valid_rows = valid_flag.astype(jnp.float32)[:, None]
    cosine, sine_table = rope_tables(position, HEAD_DIM)
    inputs = tokens.astype(jnp.float32)
    gains_all = gains_low.astype(jnp.float32)
    normed, norm_back_one = jax.vjp(normalize, inputs, gains_all[:D])
    normed_low = normed.astype(jnp.bfloat16)
    projected = jnp.dot(normed_low, w_qkv, preferred_element_type=jnp.float32) + biases_low.astype(
        jnp.float32
    )
    queries = projected[:, :D].reshape(row_count, HEADS, HEAD_DIM)
    keys_pre = projected[:, D : D + kv_width].reshape(row_count, KV_HEADS, HEAD_DIM)
    values_low = (
        projected[:, D + kv_width :].reshape(row_count, KV_HEADS, HEAD_DIM).astype(jnp.bfloat16)
    )
    (queries_rot, keys_rot), rope_back = jax.vjp(
        lambda query_in, key_in: (
            rotate(query_in, cosine, sine_table),
            rotate(key_in, cosine, sine_table),
        ),
        queries,
        keys_pre,
    )
    queries_low = queries_rot.astype(jnp.bfloat16).reshape(row_count, KV_HEADS, repeat, HEAD_DIM)
    keys_low = keys_rot.astype(jnp.bfloat16)
    key_index = jnp.arange(row_count, dtype=jnp.int32)

    def block_scores(offset):
        raw_scores = (
            jnp.einsum("qgrd,kgd->grqk", queries_low, keys_low, preferred_element_type=jnp.float32)
            * scaling
        )
        allowed = (segment[offset : offset + block_rows, None] == segment[None, :]) & (
            key_index[None, :] <= key_index[:, None]
        )
        return jnp.where(allowed[None, None], raw_scores, MASKED)

    offsets = list(range(0, row_count, block_rows))
    attended_parts, log_parts = ([], [])
    for offset in offsets:
        scores = block_scores(offset)
        highest = jnp.max(scores, axis=-1, keepdims=True)
        exponent = jnp.exp(scores - highest)
        totals = jnp.sum(exponent, axis=-1, keepdims=True)
        soft_low = (exponent / totals).astype(jnp.bfloat16)
        attended_parts.append(
            jnp.einsum("grqk,kgd->qgrd", soft_low, values_low, preferred_element_type=jnp.float32)
        )
        log_parts.append(highest + jnp.log(totals))
    attended = attended_parts[0].reshape(row_count, D).astype(jnp.bfloat16)
    hidden = inputs + jnp.dot(attended, w_out, preferred_element_type=jnp.float32)
    normed_two, norm_back_two = jax.vjp(normalize, hidden, gains_all[D:])
    normed_two_low = normed_two.astype(jnp.bfloat16)
    expanded = jnp.dot(normed_two_low, w_expand, preferred_element_type=jnp.float32)
    activated, gate_back = jax.vjp(swiglu, expanded)
    activated_low = activated.astype(jnp.bfloat16)
    result = hidden + jnp.dot(activated_low, w_down, preferred_element_type=jnp.float32)
    output = (result * valid_rows).astype(jnp.bfloat16)
    upstream = cotangent.astype(jnp.float32) * valid_rows
    upstream_low = upstream.astype(jnp.bfloat16)
    grad_down = jnp.einsum(
        "nf,nd->fd", activated_low, upstream_low, preferred_element_type=jnp.float32
    )
    back_act = jnp.einsum("nd,fd->nf", upstream_low, w_down, preferred_element_type=jnp.float32)
    back_expand = gate_back(back_act)[0].astype(jnp.bfloat16)
    grad_expand = jnp.einsum(
        "nd,nf->df", normed_two_low, back_expand, preferred_element_type=jnp.float32
    )
    back_normed_two = jnp.einsum(
        "nf,df->nd", back_expand, w_expand, preferred_element_type=jnp.float32
    )
    back_hidden_part, grad_gain_two = norm_back_two(back_normed_two)
    back_hidden = upstream + back_hidden_part
    back_branch = back_hidden.astype(jnp.bfloat16)
    grad_out = jnp.einsum("nd,ne->de", attended, back_branch, preferred_element_type=jnp.float32)
    back_attended = jnp.einsum("ne,de->nd", back_branch, w_out, preferred_element_type=jnp.float32)
    back_attended = back_attended.astype(jnp.bfloat16).reshape(
        row_count, KV_HEADS, repeat, HEAD_DIM
    )
    query_grads = []
    key_grad = jnp.zeros((row_count, KV_HEADS, HEAD_DIM), jnp.float32)
    value_grad = jnp.zeros((row_count, KV_HEADS, HEAD_DIM), jnp.float32)
    for position_block, offset in enumerate(offsets):
        scores = block_scores(offset)
        soft_weights = jnp.exp(scores - log_parts[position_block])
        back_soft = jnp.einsum(
            "qgrd,kgd->grqk", back_attended, values_low, preferred_element_type=jnp.float32
        )
        inner_sum = jnp.sum(soft_weights * back_soft, axis=-1, keepdims=True)
        back_scores = (soft_weights * (back_soft - inner_sum)).astype(jnp.bfloat16)
        query_grads.append(
            jnp.einsum("grqk,kgd->qgrd", back_scores, keys_low, preferred_element_type=jnp.float32)
            * scaling
        )
        key_grad = (
            jnp.einsum(
                "grqk,qgrd->kgd", back_scores, queries_low, preferred_element_type=jnp.float32
            )
            * scaling
        )
        value_grad = jnp.einsum(
            "grqk,qgrd->kgd",
            soft_weights.astype(jnp.bfloat16),
            back_attended,
            preferred_element_type=jnp.float32,
        )
    back_queries = query_grads[0].reshape(row_count, HEADS, HEAD_DIM)
    back_query_pre, back_key_pre = rope_back((back_queries, key_grad))
    back_projected = jnp.concatenate(
        [
            back_query_pre.reshape(row_count, D),
            back_key_pre.reshape(row_count, kv_width),
            value_grad.reshape(row_count, kv_width),
        ],
        axis=1,
    ).astype(jnp.bfloat16)
    grad_biases = jnp.sum(back_projected, axis=0, dtype=jnp.float32)
    grad_qkv = jnp.einsum(
        "nd,ne->de", normed_low, back_projected, preferred_element_type=jnp.float32
    )
    back_normed = jnp.einsum("ne,de->nd", back_projected, w_qkv, preferred_element_type=jnp.float32)
    back_inputs, grad_gain_one = norm_back_one(back_normed)
    token_grad = (back_hidden + back_inputs).astype(jnp.bfloat16)
    groups = lax.axis_size("group")
    data_size = lax.axis_size("dp")
    local_grads = (
        grad_qkv,
        grad_out,
        grad_expand,
        grad_down,
        jnp.concatenate([grad_gain_one, grad_gain_two]),
        grad_biases,
    )
    flat_grads = jnp.concatenate(
        [piece_now.reshape(groups, -1) for piece_now in local_grads], axis=1
    )
    flat_width = flat_grads.shape[1]
    padded = -(-flat_width // data_size) * data_size
    arranged = jnp.pad(flat_grads, ((0, 0), (0, padded - flat_width))).reshape(
        groups, data_size, padded // data_size
    )
    arranged = jnp.transpose(arranged, (1, 0, 2)).reshape(data_size * groups, padded // data_size)
    piece_sum = lax.psum_scatter(arranged, ("dp", "group"), scatter_dimension=0, tiled=True)
    owned = lax.all_gather(piece_sum, "dp", axis=0, tiled=True).reshape(-1)[:flat_width]
    rates = (RATE_MATRIX, RATE_OUT, RATE_MATRIX, RATE_MATRIX, RATE_VECTOR, RATE_VECTOR)
    decays = (DECAY, DECAY, DECAY, DECAY, 0.0, 0.0)
    grads_low, updated, momenta, variances = ([], [], [], [])
    cursor = 0
    for master, first_old, second_old, step_rate, decay_rate in zip(
        masters, firsts, seconds, rates, decays
    ):
        gradient = owned[cursor : cursor + master.size].reshape(master.shape)
        cursor = cursor + master.size
        weight_new, first_new, second_new = adamw(
            master, first_old, second_old, gradient, step_rate, decay_rate
        )
        grads_low.append(gradient.astype(jnp.bfloat16))
        updated.append(weight_new)
        momenta.append(first_new)
        variances.append(second_new)
    return (
        output,
        token_grad,
        grads_low[0],
        grads_low[1],
        grads_low[2],
        grads_low[3],
        grads_low[4],
        grads_low[5],
        updated[0],
        updated[1],
        updated[2],
        updated[3],
        updated[4],
        updated[5],
        momenta[0],
        momenta[1],
        momenta[2],
        momenta[3],
        momenta[4],
        momenta[5],
        variances[0],
        variances[1],
        variances[2],
        variances[3],
        variances[4],
        variances[5],
    )


def solution(mesh):
    in_specs = (
        P(("dp", "group"), None),
        P(("dp", "group"), None),
        P(("dp", "group"), None),
        P("group", None),
        P("group", None),
        P("group", None),
        P("group", None),
        P("group"),
        P("group"),
        P("group", None),
        P("group", None),
        P("group", None),
        P("group", None),
        P("group"),
        P("group"),
        P("group", None),
        P("group", None),
        P("group", None),
        P("group", None),
        P("group"),
        P("group"),
    )
    out_specs = (
        P(("dp", "group"), None),
        P(("dp", "group"), None),
        P("group", None),
        P("group", None),
        P("group", None),
        P("group", None),
        P("group"),
        P("group"),
        P("group", None),
        P("group", None),
        P("group", None),
        P("group", None),
        P("group"),
        P("group"),
        P("group", None),
        P("group", None),
        P("group", None),
        P("group", None),
        P("group"),
        P("group"),
        P("group", None),
        P("group", None),
        P("group", None),
        P("group", None),
        P("group"),
        P("group"),
    )
    return jax.shard_map(local, mesh=mesh, in_specs=in_specs, out_specs=out_specs, check_vma=False)
```

profile of v0, /device:TPU:0, one launch (start us, length us, event | category | flops | bytes accessed | tf_op | source)
XLA Modules:
  0.0 2418.8 jit_solution(16864654719189626343)
XLA Ops:
  7.3 2.8 convert_element_type.125
  10.1 1.0 convert_element_type.135
  11.1 9.2 convert_element_type.137
  20.4 6.4 convert_element_type.139
  29.0 6.2 all-reduce.6
  35.2 4.4 all-gather
  40.5 0.7 compare_convert_fusion
  41.9 3.9 all-gather.8.cloned.1.call-done
  45.8 2.5 convolution_add_fusion
  49.2 0.7 fusion.68
  50.5 1.3 copy-done.1
  51.7 0.8 fusion.18
  52.5 23.0 all-gather.10.cloned.1.call-done
  75.5 2.2 multiply_reduce_fusion.2
  77.8 208.4 %all-gather.12.cloned.1.call-done = bf16[896,9728]{1,0:T(8,128)(2,1)} async-done(((bf16[448,9728]{1,0:T(8,128)(2,1)}), bf16[896,9728]{1,0:T(8,128)(2,1)}) %all-gather.12.cloned.1.call-update) | async-done | bytes 17432592 | tf_op jit(solution)/shard_map/all_gather | solution.py:106
  286.3 14.2 fusion.60
  300.5 97.9 %all-gather.14.cloned.1.call-done = bf16[4864,896]{1,0:T(8,128)(2,1)} async-done(((bf16[2432,896]{1,0:T(8,128)(2,1)}), bf16[4864,896]{1,0:T(8,128)(2,1)}) %all-gather.14.cloned.1.call-update) | async-done | bytes 8716304 | tf_op jit(solution)/shard_map/all_gather | solution.py:107
  398.4 13.0 fusion.39
  411.4 13.3 multiply_reduce_fusion
  424.8 1.5 fusion.31
  426.3 2.5 convolution_convert_fusion
  429.0 3.5 fusion.24
  432.6 0.8 fusion.5
  433.5 0.9 fusion.7
  434.4 1.3 fusion.20
  436.2 2.3 fusion.41
  438.5 20.3 fusion.37
  459.1 2.9 fusion.48
  462.2 7.2 reshape.299
  469.4 5.0 constant_dynamic-update-slice_fusion.5
  474.4 3.7 reshape.300
  478.2 58.3 %reshape.301 = f32[2,4358144]{1,0:T(2,128)} reshape(f32[896,9728]{1,0:T(8,128)} %fusion.37) | data formatting | bytes 69730304 | tf_op jit(solution)/shard_map/reshape | solution.py:250
  536.4 8.3 fusion.44
  544.8 25.2 %reshape.302 = f32[2,2179072]{1,0:T(2,128)} reshape(f32[4864,896]{1,0:T(8,128)} %fusion.44) | data formatting | bytes 34865152 | tf_op jit(solution)/shard_map/reshape | solution.py:250
  570.0 4.3 fusion.30
  574.5 2.2 constant_dynamic-update-slice_fusion.4
  576.7 28.1 %constant_dynamic-update-slice_fusion.3 = f32[2,7456192]{1,0:T(2,128)} fusion(f32[2,7456192]{1,0:T(2,128)} %constant_dynamic-update-slice_fusion.4, f32[2,4358144]{1,0:T(2,128)} %reshape.301), kind=kLoop, calls=%fused_computation.104 | loop fusion | bytes 69730304
  604.9 6.3 constant_dynamic-update-slice_fusion.2
  611.8 0.6 constant_dynamic-update-slice_fusion
  612.4 135.5 %reshape.332 = f32[14912384]{0:T(1024)} reshape(f32[2,7456192]{1,0:T(2,128)} %constant_dynamic-update-slice_fusion) | data formatting | bytes 119299072
  747.9 78.2 %reshape.305 = f32[2,16,466012]{2,1,0:T(8,128)} reshape(f32[14912384]{0:T(1024)} %reshape.332) | data formatting | bytes 119299072 | tf_op jit(solution)/shard_map/reshape | solution.py:254
  826.0 96.6 %copy.99 = f32[16,2,466012]{2,1,0:T(2,128)} copy(f32[16,2,466012]{2,0,1:T(8,128)} %bitcast.79) | data formatting | bytes 119299072 | tf_op jit(solution)/shard_map/transpose | solution.py:257
  922.6 90.4 %reshape.306 = f32[32,466012]{1,0:T(8,128)} reshape(f32[16,2,466012]{2,1,0:T(2,128)} %copy.99) | data formatting | bytes 119299072 | tf_op jit(solution)/shard_map/reshape | solution.py:257
  1013.2 838.1 %all-reduce.10.cloned.1.call-done = f32[32,466012]{1,0:T(8,128)} async-done(((f32[32,466012]{1,0:T(8,128)}), f32[32,466012]{1,0:T(8,128)}) %all-reduce.10.cloned.1.call-update) | async-done | bytes 59649552
  1851.4 7.3 dynamic-slice_bitcast_fusion
  1858.8 1.1 fusion.33
  1859.8 7.8 fusion.17
  1867.6 141.6 %all-gather.16.cloned.1.call-done = f32[16,1,466012]{2,1,0:T(1,128)} async-done(((f32[1,1,466012]{2,1,0:T(1,128)}), f32[16,1,466012]{2,1,0:T(1,128)}) %all-gather.16.cloned.1.call-update) | async-done | bytes 29824784 | tf_op jit(solution)/shard_map/all_gather | solution.py:259
  2009.2 218.6 %reduce.2 = f32[16,466012]{1,0:T(8,128)} reduce(f32[16,1,466012]{2,1,0:T(1,128)} %all-gather.16.cloned.1.call-done, f32[]{:T(128)} %constant.63), dimensions={1}, to_apply=%all-gather.1.reduce_sub_computation | reduce | bytes 59649540 | tf_op jit(solution)/shard_map/all_gather | solution.py:259
  2227.8 39.3 %reshape.307 = f32[7456192]{0:T(1024)} reshape(f32[16,466012]{1,0:T(8,128)} %reduce.2) | data formatting | bytes 59649536 | tf_op jit(solution)/shard_map/reshape | solution.py:259
  2267.1 2.7 slice.88
  2269.8 14.0 slice.89
  2283.8 6.8 copy-done
  2290.6 3.7 slice.90
  2295.4 1.7 reshape.308
  2297.1 2.6 reshape.309
  2299.7 18.1 reshape.310
  2317.9 10.4 reshape.311
  2328.4 1.3 multiply_subtract_fusion.5
  2329.7 1.3 multiply_subtract_fusion.4
  2331.0 7.6 multiply_subtract_fusion.2
  2338.6 3.3 multiply_subtract_fusion.3
  2341.9 48.1 %multiply_subtract_fusion = (f32[448,9728]{1,0:T(8,128)}, f32[448,9728]{1,0:T(8,128)}, f32[448,9728]{1,0:T(8,128)}, bf16[448,9728]{1,0:T(8,128)(2,1)}) fusion(f32[448,9728]{1,0:T(8,128)} %param.26, f32[448,9728]{1,0:T(8,128)} %reshape.310, f32[448,9728]{1,0:T(8,128)} %param.32, f32[448,9728]{1,0:T(8,128)} %param.38), kind=kLoop, calls=%fused_computation.2 | loop fusion | flops 69730304 | bytes 130744320 | tf_op jit(solution)/shard_map/sub | solution.py:74
  2390.1 21.6 multiply_subtract_fusion.1
  (182 shorter events, 7.9 us)
Async XLA Ops:
  7.2 2.9 copy-start.12
  7.2 38.6 %all-gather.8.cloned.1.call-start = ((), (), s32[]{:S(2)}) async-start(), calls=%async_computation | async-start | bytes 3096576 | tf_op jit(solution)/shard_map/all_gather | solution.py:104
  10.0 65.5 %all-gather.10.cloned.1.call-start = ((), (), s32[]{:S(2)}) async-start(), calls=%async_computation.1 | async-start | bytes 2408448 | tf_op jit(solution)/shard_map/all_gather | solution.py:105
  11.1 275.2 %all-gather.12.cloned.1.call-start = ((), (), s32[]{:S(2)}) async-start(), calls=%async_computation.2 | async-start | bytes 26148864 | tf_op jit(solution)/shard_map/all_gather | solution.py:106
  20.4 378.0 %all-gather.14.cloned.1.call-start = ((), (), s32[]{:S(2)}) async-start(), calls=%async_computation.3 | async-start | bytes 13074432 | tf_op jit(solution)/shard_map/all_gather | solution.py:107
  26.8 8.4 copy-start.38
  26.8 12.8 copy-start.51
  26.8 14.6 copy-start.9
  26.8 1824.5 %all-reduce.10.cloned.1.call-start = ((), (), s32[]{:S(2)}) async-start(), calls=%async_computation.5 | async-start | bytes 119308288
  41.2 495.3 %copy-start.44 = (f32[256]{0:T(256)}, f32[256]{0:T(256)S(1)}, u32[]{:S(2)}) copy-start(f32[256]{0:T(256)S(1)} %compare_convert_fusion) | copy-start | bytes 3076
  41.2 528.8 %copy-start.30 = (f32[896]{0:T(1024)}, f32[896]{0:T(1024)S(1)}, u32[]{:S(2)}) copy-start(f32[896]{0:T(1024)S(1)} %get-tuple-element.31) | copy-start | bytes 10756
  41.6 6.8 copy-start.42
  41.6 528.4 %copy-start.36 = (f32[256]{0:T(256)}, f32[256]{0:T(256)S(1)}, u32[]{:S(2)}) copy-start(f32[256]{0:T(256)S(1)} %fusion.53) | copy-start | bytes 3076
  48.5 1.9 copy-start.28
  49.0 1.5 copy-start.32
  49.2 3.4 copy-start.23
  49.9 1.8 copy-start.1
  52.5 247.9 %copy-start.17 = (bf16[2,64,7,256]{3,1,2,0:T(8,128)(2,1)}, bf16[2,64,7,256]{3,1,2,0:T(8,128)(2,1)S(1)}, u32[]{:S(2)}) copy-start(bf16[2,64,7,256]{3,1,2,0:T(8,128)(2,1)S(1)} %fusion.18) | copy-start | bytes 1376260
  77.8 360.8 %copy-start.3 = (f32[256,896]{1,0:T(8,128)}, f32[256,896]{1,0:T(8,128)S(1)}, u32[]{:S(2)}) copy-start(f32[256,896]{1,0:T(8,128)S(1)} %get-tuple-element.70) | copy-start | bytes 2752516
  286.3 112.1 %copy-start.19 = (bf16[256,896]{1,0:T(8,128)(2,1)S(1)}, bf16[256,896]{1,0:T(8,128)(2,1)}, u32[]{:S(2)}) copy-start(bf16[256,896]{1,0:T(8,128)(2,1)} %param.22) | copy-start | bytes 1376260
  426.3 9.9 copy-start.5
  429.0 3.5 copy-start.2
  429.0 3.5 copy-start.29
  433.4 2.3 copy-start.33
  433.4 2.3 copy-start.35
  434.4 1.8 copy-start.18
  438.5 20.3 copy-start.27
  438.5 20.5 copy-start.26
  459.1 2.9 copy-start.15
  469.4 5.0 copy-start.7
  478.2 58.3 %copy-start.16 = (bf16[256,4864]{1,0:T(8,128)(2,1)S(1)}, bf16[256,4864]{1,0:T(8,128)(2,1)}, u32[]{:S(2)}) copy-start(bf16[256,4864]{1,0:T(8,128)(2,1)} %get-tuple-element.53) | copy-start | bytes 7471108
  478.2 58.3 %copy-start.20 = (bf16[256,896]{1,0:T(8,128)(2,1)S(1)}, bf16[256,896]{1,0:T(8,128)(2,1)}, u32[]{:S(2)}) copy-start(bf16[256,896]{1,0:T(8,128)(2,1)} %param.22) | copy-start | bytes 1376260
  570.0 4.4 copy-start.8
  574.5 30.4 %slice-start.1 = ((s8[17432576]{0:T(1024)(128)(4,1)}), s8[4194304]{0:T(1024)(128)(4,1)S(1)}, s32[]{:S(2)}) async-start(s8[17432576]{0:T(1024)(128)(4,1)} %bitcast.80), calls=%async_computation.7 | async-start | bytes 8388608
  576.7 28.1 %slice-start.2 = ((s8[17432576]{0:T(1024)(128)(4,1)}), s8[4194304]{0:T(1024)(128)(4,1)S(1)}, s32[]{:S(2)}) async-start(s8[17432576]{0:T(1024)(128)(4,1)} %bitcast.80), calls=%async_computation.8 | async-start | bytes 8388608
  576.7 28.2 %slice-start.3 = ((s8[17432576]{0:T(1024)(128)(4,1)}), s8[4194304]{0:T(1024)(128)(4,1)S(1)}, s32[]{:S(2)}) async-start(s8[17432576]{0:T(1024)(128)(4,1)} %bitcast.80), calls=%async_computation.9 | async-start | bytes 8388608
  576.7 28.2 %slice-start.4 = ((s8[17432576]{0:T(1024)(128)(4,1)}), s8[4194304]{0:T(1024)(128)(4,1)S(1)}, s32[]{:S(2)}) async-start(s8[17432576]{0:T(1024)(128)(4,1)} %bitcast.80), calls=%async_computation.10 | async-start | bytes 8388608
  576.7 28.2 %slice-start.5 = ((s8[17432576]{0:T(1024)(128)(4,1)}), s8[655360]{0:T(1024)(128)(4,1)S(1)}, s32[]{:S(2)}) async-start(s8[17432576]{0:T(1024)(128)(4,1)} %bitcast.80), calls=%async_computation.11 | async-start | bytes 1310720
  1013.1 845.6 %copy-start.43 = (f32[256]{0:T(256)S(1)}, f32[256]{0:T(256)}, u32[]{:S(2)}) copy-start(f32[256]{0:T(256)} %copy-done.42) | copy-start | bytes 3076
  1013.1 845.6 %copy-start.50 = (f32[256]{0:T(256)S(1)}, f32[256]{0:T(256)}, u32[]{:S(2)}) copy-start(f32[256]{0:T(256)} %get-tuple-element.29) | copy-start | bytes 3076
  1013.1 845.6 %copy-start.6 = (f32[256,896]{1,0:T(8,128)S(1)}, f32[256,896]{1,0:T(8,128)}, u32[]{:S(2)}) copy-start(f32[256,896]{1,0:T(8,128)} %copy-done.5) | copy-start | bytes 2752516
  1013.1 845.6 %copy-start.10 = (bf16[256,896]{1,0:T(8,128)(2,1)S(1)}, bf16[256,896]{1,0:T(8,128)(2,1)}, u32[]{:S(2)}) copy-start(bf16[256,896]{1,0:T(8,128)(2,1)} %param.21) | copy-start | bytes 1376260
  1013.1 845.6 %copy-start.25 = (f32[256,896]{1,0:T(8,128)S(1)}, f32[256,896]{1,0:T(8,128)}, u32[]{:S(2)}) copy-start(f32[256,896]{1,0:T(8,128)} %get-tuple-element.74) | copy-start | bytes 2752516
  1013.1 845.6 %copy-start.31 = (f32[896]{0:T(1024)S(1)}, f32[896]{0:T(1024)}, u32[]{:S(2)}) copy-start(f32[896]{0:T(1024)} %copy-done.30) | copy-start | bytes 10756
  1013.1 845.6 %copy-start.37 = (f32[256]{0:T(256)S(1)}, f32[256]{0:T(256)}, u32[]{:S(2)}) copy-start(f32[256]{0:T(256)} %copy-done.36) | copy-start | bytes 3076
  1013.2 996.0 %all-gather.16.cloned.1.call-start = ((), (), s32[]{:S(2)}) async-start(), calls=%async_computation.4 | async-start | bytes 31691264 | tf_op jit(solution)/shard_map/all_gather | solution.py:259
  1013.2 846.6 %copy-start.4 = (f32[256,896]{1,0:T(8,128)S(1)}, f32[256,896]{1,0:T(8,128)}, u32[]{:S(2)}) copy-start(f32[256,896]{1,0:T(8,128)} %copy-done.3) | copy-start | bytes 2752516
  1013.2 846.6 %copy-start.45 = (f32[256]{0:T(256)S(1)}, f32[256]{0:T(256)}, u32[]{:S(2)}) copy-start(f32[256]{0:T(256)} %copy-done.44) | copy-start | bytes 3076
  2269.8 20.8 copy-start
  2290.6 4.9 slice-start
  2317.8 10.5 copy-start.39
  2317.8 10.5 copy-start.46
  2317.8 10.5 copy-start.47
  2317.8 11.8 copy-start.41
  2317.9 11.8 copy-start.48
  2317.9 11.8 copy-start.49
  2317.9 13.1 copy-start.11
  2331.0 7.6 copy-start.13
  2331.0 7.6 copy-start.14
  2331.0 7.6 copy-start.21
  2331.0 7.6 copy-start.22
  2338.6 51.4 %slice-start.6 = ((s8[8716288]{0:T(1024)(128)(4,1)}), s8[4194304]{0:T(1024)(128)(4,1)S(1)}, s32[]{:S(2)}) async-start(s8[8716288]{0:T(1024)(128)(4,1)} %bitcast.82), calls=%async_computation.12 | async-start | bytes 8388608
  2341.9 48.2 %slice-start.7 = ((s8[8716288]{0:T(1024)(128)(4,1)}), s8[4194304]{0:T(1024)(128)(4,1)S(1)}, s32[]{:S(2)}) async-start(s8[8716288]{0:T(1024)(128)(4,1)} %bitcast.82), calls=%async_computation.13 | async-start | bytes 8388608
  2341.9 48.2 %slice-start.8 = ((s8[8716288]{0:T(1024)(128)(4,1)}), s8[327680]{0:T(1024)(128)(4,1)S(1)}, s32[]{:S(2)}) async-start(s8[8716288]{0:T(1024)(128)(4,1)} %bitcast.82), calls=%async_computation.14 | async-start | bytes 655360
  (4 other events, 3.8 us)
Sparse Core Ops, SparseCore 0:
  10.2 35.6 all-gather.7
  47.9 27.5 all-gather.9
  77.7 208.5 all-gather.11
  288.3 110.0 all-gather.13
  1013.2 838.1 all-reduce.9
  1858.8 150.3 all-gather.15
where the time goes:
time: 2430 us; the launch traced here: 2420 us
  waiting for transfers between devices  1310 us (54%)
  local copies, waits for them, and re-layouts  650 us (27%)
  other arithmetic  327 us (13%)
  matrix products  101 us (4%)
    unnamed x7, waiting for transfers between devices  838 us
    all_gather x1, other arithmetic, local(): lax.all_gather(piece_sum, 'dp', axis=0, tiled=True).reshape(-1)[:flat_width]  219 us
    all_gather x1, waiting for transfers between devices, local(): lax.all_gather(expand_weight.astype(jnp.bfloat16), 'group', axis=0, tiled...  208 us
    unnamed x133, local copies, waits for them, and re-layouts  195 us
    all_gather x1, waiting for transfers between devices, local(): lax.all_gather(piece_sum, 'dp', axis=0, tiled=True).reshape(-1)[:flat_width]  142 us
    all_gather x1, waiting for transfers between devices, local(): lax.all_gather(down_weight.astype(jnp.bfloat16), 'group', axis=0, tiled=T...  97.9 us
    transpose x1, local copies, waits for them, and re-layouts, local(): jnp.transpose(arranged, (1, 0, 2))  96.6 us
    reshape x6, local copies, waits for them, and re-layouts, local(): piece_now.reshape(groups, -1)  94.5 us
  transfers between devices with their start and end apart: 6, of which 6 were waited for; matrix products, arithmetic and copies ran while one was open for 2% of the time, Pallas kernels for 0%

commit v1 on v0

--- a/solution.py
+++ b/solution.py
@@ -56,11 +56,6 @@
 def normalize(values, gain_row):
     scaling = lax.rsqrt(jnp.mean(values * values, axis=-1, keepdims=True) + EPS_NORM)
     return values * scaling * gain_row
-
-
-def swiglu(expanded):
-    half_cols = expanded.shape[1] // 2
-    return jax.nn.silu(expanded[:, :half_cols]) * expanded[:, half_cols:]
 
 
 def adamw(master, first_old, second_old, gradient, step_rate, decay_rate):
@@ -100,14 +95,59 @@
     masters = (qkv_weight, out_weight, expand_weight, down_weight, norm_gains, qkv_biases)
     firsts = (qkv_first, out_first, expand_first, down_first, gains_first, biases_first)
     seconds = (qkv_second, out_second, expand_second, down_second, gains_second, biases_second)
-    w_qkv, w_out, w_expand, w_down, gains_low, biases_low = (
-        lax.all_gather(qkv_weight.astype(jnp.bfloat16), "group", axis=0, tiled=True),
-        lax.all_gather(out_weight.astype(jnp.bfloat16), "group", axis=0, tiled=True),
-        lax.all_gather(expand_weight.astype(jnp.bfloat16), "group", axis=0, tiled=True),
-        lax.all_gather(down_weight.astype(jnp.bfloat16), "group", axis=0, tiled=True),
-        lax.all_gather(norm_gains.astype(jnp.bfloat16), "group", axis=0, tiled=True),
-        lax.all_gather(qkv_biases.astype(jnp.bfloat16), "group", axis=0, tiled=True),
-    )
+    groups = lax.axis_size("group")
+    data_size = lax.axis_size("dp")
+    member = lax.axis_index("dp")
+    row_parts = data_size // 2
+    col_part, row_part = member // row_parts, member % row_parts
+    attn_cols = (qkv_weight.shape[1] + out_weight.shape[1]) // 2
+    qkv_tail = qkv_weight.shape[1] - attn_cols
+    shard_rows = out_weight.shape[0]
+    piece_rows = shard_rows // row_parts
+    both = ("dp", "group")
+
+    def own_piece(left, right):
+        start = row_part * piece_rows
+        return jnp.where(
+            col_part == 0,
+            lax.dynamic_slice_in_dim(left, start, piece_rows, 0),
+            lax.dynamic_slice_in_dim(right, start, piece_rows, 0),
+        ).astype(jnp.bfloat16)
+
+    def deal(values):
+        rows = values.shape[0]
+        split = values.reshape(rows, groups, row_parts, piece_rows)
+        return jnp.swapaxes(split, 1, 2).reshape(rows, D)
+
+    def undeal(values):
+        rows = values.shape[0]
+        split = values.reshape(rows, row_parts, groups, piece_rows)
+        return jnp.swapaxes(split, 1, 2).reshape(rows, D)
+
+    def scatter_sum(partial):
+        return lax.psum_scatter(partial, both, scatter_dimension=0, tiled=True)
+
+    attn_piece = own_piece(
+        qkv_weight[:, :attn_cols], jnp.concatenate([qkv_weight[:, attn_cols:], out_weight], axis=1)
+    )
+    w_attn = lax.all_gather(attn_piece, both, axis=0, tiled=True)
+    half_ff = expand_weight.shape[1] // 2
+    expand_piece = own_piece(expand_weight[:, :half_ff], expand_weight[:, half_ff:])
+    w_expand = lax.all_gather(expand_piece, both, axis=0, tiled=True)
+    down_rows = down_weight.shape[0] // data_size
+    down_piece = lax.dynamic_slice_in_dim(down_weight, member * down_rows, down_rows, 0)
+    w_down = lax.all_gather(
+        down_piece.astype(jnp.bfloat16), ("group", "dp"), axis=0, tiled=True
+    )
+    w_qkv = jnp.concatenate([w_attn[:D], w_attn[D:, :qkv_tail]], axis=1)
+    w_out = w_attn[D:, qkv_tail:]
+    w_gate, w_up = w_expand[:D], w_expand[D:]
+    vectors = lax.all_gather(
+        jnp.concatenate([norm_gains, qkv_biases]).astype(jnp.bfloat16), "group", axis=0
+    )
+    own_gains = norm_gains.shape[0]
+    gains_low = vectors[:, :own_gains].reshape(-1)
+    biases_low = vectors[:, own_gains:].reshape(-1)
     row_count = tokens.shape[0]
     block_rows = min(512, row_count)
     kv_width = KV_HEADS * HEAD_DIM
@@ -120,7 +160,8 @@
     gains_all = gains_low.astype(jnp.float32)
     normed, norm_back_one = jax.vjp(normalize, inputs, gains_all[:D])
     normed_low = normed.astype(jnp.bfloat16)
-    projected = jnp.dot(normed_low, w_qkv, preferred_element_type=jnp.float32) + biases_low.astype(
+    normed_deal = deal(normed_low)
+    projected = jnp.dot(normed_deal, w_qkv, preferred_element_type=jnp.float32) + biases_low.astype(
         jnp.float32
     )
     queries = projected[:, :D].reshape(row_count, HEADS, HEAD_DIM)
@@ -163,11 +204,14 @@
         )
         log_parts.append(highest + jnp.log(totals))
     attended = attended_parts[0].reshape(row_count, D).astype(jnp.bfloat16)
-    hidden = inputs + jnp.dot(attended, w_out, preferred_element_type=jnp.float32)
+    attended_deal = deal(attended)
+    hidden = inputs + jnp.dot(attended_deal, w_out, preferred_element_type=jnp.float32)
     normed_two, norm_back_two = jax.vjp(normalize, hidden, gains_all[D:])
     normed_two_low = normed_two.astype(jnp.bfloat16)
-    expanded = jnp.dot(normed_two_low, w_expand, preferred_element_type=jnp.float32)
-    activated, gate_back = jax.vjp(swiglu, expanded)
+    two_deal = deal(normed_two_low)
+    gate = jnp.dot(two_deal, w_gate, preferred_element_type=jnp.float32)
+    up = jnp.dot(two_deal, w_up, preferred_element_type=jnp.float32)
+    activated, gate_back = jax.vjp(lambda g, u: jax.nn.silu(g) * u, gate, up)
     activated_low = activated.astype(jnp.bfloat16)
     result = hidden + jnp.dot(activated_low, w_down, preferred_element_type=jnp.float32)
     output = (result * valid_rows).astype(jnp.bfloat16)
@@ -175,21 +219,32 @@
     upstream_low = upstream.astype(jnp.bfloat16)
     grad_down = jnp.einsum(
         "nf,nd->fd", activated_low, upstream_low, preferred_element_type=jnp.float32
-    )
+    ).astype(jnp.bfloat16)
+    piece_down = lax.psum_scatter(grad_down, ("group", "dp"), scatter_dimension=0, tiled=True)
     back_act = jnp.einsum("nd,fd->nf", upstream_low, w_down, preferred_element_type=jnp.float32)
-    back_expand = gate_back(back_act)[0].astype(jnp.bfloat16)
-    grad_expand = jnp.einsum(
-        "nd,nf->df", normed_two_low, back_expand, preferred_element_type=jnp.float32
-    )
-    back_normed_two = jnp.einsum(
-        "nf,df->nd", back_expand, w_expand, preferred_element_type=jnp.float32
+    back_gate, back_up = (part.astype(jnp.bfloat16) for part in gate_back(back_act))
+    grad_expand = jnp.concatenate(
+        [
+            jnp.einsum("nd,nf->df", two_deal, part, preferred_element_type=jnp.float32).astype(
+                jnp.bfloat16
+            )
+            for part in (back_gate, back_up)
+        ],
+        axis=0,
+    )
+    piece_expand = scatter_sum(grad_expand)
+    back_normed_two = undeal(
+        jnp.einsum("nf,df->nd", back_gate, w_gate, preferred_element_type=jnp.float32)
+        + jnp.einsum("nf,df->nd", back_up, w_up, preferred_element_type=jnp.float32)
     )
     back_hidden_part, grad_gain_two = norm_back_two(back_normed_two)
     back_hidden = upstream + back_hidden_part
     back_branch = back_hidden.astype(jnp.bfloat16)
-    grad_out = jnp.einsum("nd,ne->de", attended, back_branch, preferred_element_type=jnp.float32)
+    grad_out = jnp.einsum(
+        "nd,ne->de", attended_deal, back_branch, preferred_element_type=jnp.float32
+    ).astype(jnp.bfloat16)
     back_attended = jnp.einsum("ne,de->nd", back_branch, w_out, preferred_element_type=jnp.float32)
-    back_attended = back_attended.astype(jnp.bfloat16).reshape(
+    back_attended = undeal(back_attended.astype(jnp.bfloat16)).reshape(
         row_count, KV_HEADS, repeat, HEAD_DIM
     )
     query_grads = []
@@ -231,41 +286,47 @@
     ).astype(jnp.bfloat16)
     grad_biases = jnp.sum(back_projected, axis=0, dtype=jnp.float32)
     grad_qkv = jnp.einsum(
-        "nd,ne->de", normed_low, back_projected, preferred_element_type=jnp.float32
-    )
-    back_normed = jnp.einsum("ne,de->nd", back_projected, w_qkv, preferred_element_type=jnp.float32)
+        "nd,ne->de", normed_deal, back_projected, preferred_element_type=jnp.float32
+    ).astype(jnp.bfloat16)
+    grad_attn = jnp.concatenate(
+        [
+            grad_qkv[:, :attn_cols],
+            jnp.concatenate([grad_qkv[:, attn_cols:], grad_out], axis=1),
+        ],
+        axis=0,
+    )
+    piece_attn = scatter_sum(grad_attn)
+    back_normed = undeal(
+        jnp.einsum("ne,de->nd", back_projected, w_qkv, preferred_element_type=jnp.float32)
+    )
     back_inputs, grad_gain_one = norm_back_one(back_normed)
     token_grad = (back_hidden + back_inputs).astype(jnp.bfloat16)
-    groups = lax.axis_size("group")
-    data_size = lax.axis_size("dp")
-    local_grads = (
-        grad_qkv,
-        grad_out,
-        grad_expand,
-        grad_down,
-        jnp.concatenate([grad_gain_one, grad_gain_two]),
-        grad_biases,
-    )
-    flat_grads = jnp.concatenate(
-        [piece_now.reshape(groups, -1) for piece_now in local_grads], axis=1
-    )
-    flat_width = flat_grads.shape[1]
-    padded = -(-flat_width // data_size) * data_size
-    arranged = jnp.pad(flat_grads, ((0, 0), (0, padded - flat_width))).reshape(
-        groups, data_size, padded // data_size
-    )
-    arranged = jnp.transpose(arranged, (1, 0, 2)).reshape(data_size * groups, padded // data_size)
-    piece_sum = lax.psum_scatter(arranged, ("dp", "group"), scatter_dimension=0, tiled=True)
-    owned = lax.all_gather(piece_sum, "dp", axis=0, tiled=True).reshape(-1)[:flat_width]
+    small = jnp.concatenate(
+        [
+            jnp.concatenate([grad_gain_one, grad_gain_two]).reshape(groups, -1),
+            grad_biases.reshape(groups, -1),
+        ],
+        axis=1,
+    )
+    small = lax.psum(small, both)[lax.axis_index("group")]
+    own_down = lax.all_gather(piece_down, "dp", axis=0, tiled=True)
+    own_expand = lax.all_gather(piece_expand, "dp", axis=0, tiled=True)
+    own_attn = lax.all_gather(piece_attn, "dp", axis=0, tiled=True)
+    owned = (
+        jnp.concatenate([own_attn[:shard_rows], own_attn[shard_rows:, :qkv_tail]], axis=1),
+        own_attn[shard_rows:, qkv_tail:],
+        jnp.concatenate([own_expand[:shard_rows], own_expand[shard_rows:]], axis=1),
+        own_down,
+        small[:own_gains],
+        small[own_gains:],
+    )
     rates = (RATE_MATRIX, RATE_OUT, RATE_MATRIX, RATE_MATRIX, RATE_VECTOR, RATE_VECTOR)
     decays = (DECAY, DECAY, DECAY, DECAY, 0.0, 0.0)
     grads_low, updated, momenta, variances = ([], [], [], [])
-    cursor = 0
-    for master, first_old, second_old, step_rate, decay_rate in zip(
-        masters, firsts, seconds, rates, decays
+    for master, first_old, second_old, gradient_low, step_rate, decay_rate in zip(
+        masters, firsts, seconds, owned, rates, decays
     ):
-        gradient = owned[cursor : cursor + master.size].reshape(master.shape)
-        cursor = cursor + master.size
+        gradient = gradient_low.astype(jnp.float32)
         weight_new, first_new, second_new = adamw(
             master, first_old, second_old, gradient, step_rate, decay_rate
         )

time: 2430 us -> 1240 us (0.51)
  local copies, waits for them, and re-layouts: 650 us -> 33.9 us
  waiting for transfers between devices: 1310 us -> 947 us
  other arithmetic: 327 us -> 105 us
  blocking collectives: 10.6 us -> 46.2 us
    unnamed x7 -> x10, waiting for transfers between devices: 838 us -> 164 us
    reduce_scatter x0 -> x2, waiting for transfers between devices: none -> 480 us  [scatter_sum(): return lax.psum_scatter(partial, both, scatter_dimension=0, tiled=True)]
    reshape x13 -> x4, local copies, waits for them, and re-layouts: 335 us -> 1.87 us  [the longest x2 1.78 us: undeal(): return jnp.swapaxes(split, 1, 2).reshape(rows, D)]
    all_gather x1 -> x0, other arithmetic: 219 us -> none  [local(): lax.all_gather(piece_sum, 'dp', axis=0, tiled=True).reshape(-1)[:flat_width]]
    unnamed x133 -> x112, local copies, waits for them, and re-layouts: 195 us -> 5.32 us
    all_gather x5 -> x6, waiting for transfers between devices: 475 us -> 303 us  [the longest x1 110 us: local(): w_expand = lax.all_gather(expand_piece, both, axis=0, tiled=True)]
    transpose x1 -> x5, local copies, waits for them, and re-layouts: 96.6 us -> 1.15 us  [the longest x3 1.09 us: undeal(): return jnp.swapaxes(split, 1, 2).reshape(rows, D)]
    psum x0 -> x1, blocking collectives: none -> 40.9 us  [local(): small = lax.psum(small, both)[lax.axis_index('group')]]
  transfers between devices with their start and end apart: 6 -> 9, of which waited for: 6 -> 8; matrix products, arithmetic and copies ran while one was open for 2% -> 9% of each run, Pallas kernels for 0% -> 0%
where the time goes in v1:
time: 1240 us; the launch traced here: 1230 us
  waiting for transfers between devices  947 us (76%)
  other arithmetic  105 us (8%)
  matrix products  77.1 us (6%)
  blocking collectives  46.2 us (4%)
  local copies, waits for them, and re-layouts  33.9 us (3%)
  between operations  15.2 us (1%)
    reduce_scatter x2, waiting for transfers between devices, scatter_sum(): return lax.psum_scatter(partial, both, scatter_dimension=0, tiled=True)  480 us
    unnamed x10, waiting for transfers between devices  164 us
    all_gather x1, waiting for transfers between devices, local(): w_expand = lax.all_gather(expand_piece, both, axis=0, tiled=True)  110 us
    sub x6, other arithmetic, adamw(): master - step_rate * (direction + decay_rate * master)  72.8 us
    all_gather x1, waiting for transfers between devices, local(): lax.all_gather(down_piece.astype(jnp.bfloat16), ('group', 'dp'), axis=0,...  69.8 us
    all_gather x1, waiting for transfers between devices, local(): own_expand = lax.all_gather(piece_expand, 'dp', axis=0, tiled=True)  55.8 us
    psum x1, blocking collectives, local(): small = lax.psum(small, both)[lax.axis_index('group')]  40.9 us
    all_gather x1, waiting for transfers between devices, local(): w_attn = lax.all_gather(attn_piece, both, axis=0, tiled=True)  39.4 us
  transfers between devices with their start and end apart: 9, of which 8 were waited for; matrix products, arithmetic and copies ran while one was open for 9% of the time, Pallas kernels for 0%

profile of v1, /device:TPU:0, one launch (start us, length us, event | category | flops | bytes accessed | tf_op | source)
XLA Modules:
  0.0 1225.2 jit_solution(8355430178394849299)
XLA Ops:
  7.3 1.0 slice.108
  8.2 1.6 slice.107
  9.9 1.6 fusion.66
  11.6 1.8 dynamic-slice_convert_fusion
  13.5 10.3 fusion.91
  23.8 2.1 select_convert_fusion
  26.1 5.3 all-gather
  31.4 0.6 slice_reduce_fusion
  33.1 0.6 slice.126
  33.8 1.2 compare_convert_fusion
  35.5 39.4 %all-gather.8.cloned.1.call-done = bf16[1792,1024]{1,0:T(8,128)(2,1)} async-done(((bf16[56,1024]{1,0:T(8,128)(2,1)}), bf16[1792,1024]{1,0:T(8,128)(2,1)}) %all-gather.8.cloned.1.call-update) | async-done | bytes 3670032 | tf_op jit(solution)/shard_map/all_gather | solution.py:133
  74.9 1.0 slice.141
  75.9 1.7 slice.140
  77.7 0.9 convolution_add_fusion
  79.6 0.7 fusion.93
  80.4 0.5 fusion.19
  80.9 0.8 fusion.41
  82.2 2.4 multiply_reduce_fusion.2
  85.3 0.8 log_add_fusion
  86.1 69.8 %all-gather.12.cloned.1.call-done = bf16[4864,896]{1,0:T(8,128)(2,1)} async-done(((bf16[152,896]{1,0:T(8,128)(2,1)}), bf16[4864,896]{1,0:T(8,128)(2,1)}) %all-gather.12.cloned.1.call-update) | async-done | bytes 8716304 | tf_op jit(solution)/shard_map/all_gather | solution.py:139
  155.9 9.9 fusion.70
  165.8 110.2 %all-gather.10.cloned.1.call-done = bf16[1792,4864]{1,0:T(8,128)(2,1)} async-done(((bf16[56,4864]{1,0:T(8,128)(2,1)}), bf16[1792,4864]{1,0:T(8,128)(2,1)}) %all-gather.10.cloned.1.call-update) | async-done | bytes 17432592 | tf_op jit(solution)/shard_map/all_gather | solution.py:136
  276.1 5.5 fusion.6
  281.6 9.0 fusion.14
  290.6 8.0 fusion.4
  298.6 6.3 fusion.36
  305.6 1.5 multiply_reduce_fusion
  307.1 0.7 multiply_multiply_fusion.7
  307.8 1.3 fusion.57
  309.1 2.2 fusion.42
  311.6 2.9 fusion.50
  314.7 0.8 fusion.16
  315.5 0.9 fusion.18
  316.5 0.7 fusion.46
  317.6 0.6 convolution_convert_fusion.4
  318.6 0.8 convolution_convert_fusion.3
  319.7 3.7 maximum_maximum_fusion
  323.9 0.5 copy-done.17
  324.4 8.1 convolution_convert_fusion
  332.6 0.9 copy-done.5
  333.5 4.3 convolution_convert_fusion.1
  337.8 2.4 convolution_convert_fusion.2
  340.3 13.8 %pad_maximum_fusion = bf16[1792,4864]{1,0:T(8,128)(2,1)} fusion(bf16[896,4864]{1,0:T(8,128)(2,1)S(1)} %convolution_convert_fusion.1, bf16[896,4864]{1,0:T(8,128)(2,1)S(1)} %convolution_convert_fusion.2), kind=kLoop, calls=%fused_computation.4 | loop fusion | flops 34865152 | bytes 34865152 | tf_op jit(solution)/shard_map/concatenate | solution.py:226
  354.1 107.5 %reduce-scatter.7.cloned.1.call-done = bf16[56,1024]{1,0:T(8,128)(2,1)} async-done(((bf16[1792,1024]{1,0:T(8,128)(2,1)}), bf16[56,1024]{1,0:T(8,128)(2,1)}) %reduce-scatter.7.cloned.1.call-update) | async-done | bytes 114704 | tf_op jit(solution)/shard_map/reduce_scatter | solution.py:128
  461.7 163.4 %reduce-scatter.11.cloned.1.call-done = bf16[152,896]{1,0:T(8,128)(2,1)} async-done(((bf16[4864,896]{1,0:T(8,128)(2,1)}), bf16[152,896]{1,0:T(8,128)(2,1)}) %reduce-scatter.11.cloned.1.call-update) | async-done | bytes 272400
  625.2 372.6 %reduce-scatter.9.cloned.1.call-done = bf16[56,4864]{1,0:T(8,128)(2,1)} async-done(((bf16[1792,4864]{1,0:T(8,128)(2,1)}), bf16[56,4864]{1,0:T(8,128)(2,1)}) %reduce-scatter.9.cloned.1.call-update) | async-done | bytes 544784 | tf_op jit(solution)/shard_map/reduce_scatter | solution.py:128
  997.8 2.3 fusion.35
  1000.2 1.0 copy.153
  1001.2 1.5 copy.154
  1002.7 1.3 convert_reduce_fusion
  1004.4 40.9 %psum.7 = f32[2,1472]{1,0:T(2,128)S(1)} all-reduce(f32[2,1472]{1,0:T(2,128)S(1)} %pad_maximum_fusion.10), channel_id=1, replica_groups=mesh['dp'=16,'group'=2] {'dp','group'}, use_global_device_ids=true, to_apply=%region_16.17 | all-reduce | flops 2944 | bytes 23552 | tf_op jit(solution)/shard_map/psum | solution.py:311
  1045.5 0.6 multiply_subtract_fusion.5
  1046.1 0.6 multiply_subtract_fusion.4
  1046.7 1.0 fusion.59
  1047.8 8.1 fusion.40
  1055.9 0.9 slice.157
  1056.9 5.5 multiply_subtract_fusion.3
  1062.5 4.1 multiply_subtract_fusion.2
  1066.7 28.0 %all-gather.18.cloned.1.call-done = bf16[2432,896]{1,0:T(8,128)(2,1)} async-done(((bf16[152,896]{1,0:T(8,128)(2,1)}), bf16[2432,896]{1,0:T(8,128)(2,1)}) %all-gather.18.cloned.1.call-update) | async-done | bytes 4358160 | tf_op jit(solution)/shard_map/all_gather | solution.py:312
  1094.6 22.1 %multiply_subtract_fusion.1 = (f32[2432,896]{1,0:T(8,128)}, f32[2432,896]{1,0:T(8,128)}, f32[2432,896]{1,0:T(8,128)}) fusion(f32[2432,896]{1,0:T(8,128)} %param.27, bf16[2432,896]{1,0:T(8,128)(2,1)} %all-gather.18.cloned.1.call-done, f32[2432,896]{1,0:T(8,128)} %param.33, f32[2432,896]{1,0:T(8,128)} %param.39), kind=kLoop, calls=%fused_computation.14 | loop fusion | flops 34865152 | bytes 56655872 | tf_op jit(solution)/shard_map/sub | solution.py:69
  1116.8 55.8 %all-gather.16.cloned.1.call-done = bf16[896,4864]{1,0:T(8,128)(2,1)} async-done(((bf16[56,4864]{1,0:T(8,128)(2,1)}), bf16[896,4864]{1,0:T(8,128)(2,1)}) %all-gather.16.cloned.1.call-update) | async-done | bytes 8716304 | tf_op jit(solution)/shard_map/all_gather | solution.py:313
  1172.5 4.0 fusion.92
  1176.6 39.8 %multiply_subtract_fusion = (f32[448,9728]{1,0:T(8,128)}, f32[448,9728]{1,0:T(8,128)}, f32[448,9728]{1,0:T(8,128)}, bf16[448,9728]{1,0:T(8,128)(2,1)}) fusion(f32[448,9728]{1,0:T(8,128)} %param.26, f32[448,9728]{1,0:T(8,128)} %param.32, f32[448,9728]{1,0:T(8,128)} %param.38, bf16[448,4864]{1,0:T(8,128)(2,1)S(1)} %get-tuple-element.59, ...), kind=kLoop, calls=%fused_computation.5 | loop fusion | flops 87162880 | bytes 122028032 | tf_op jit(solution)/shard_map/sub | solution.py:69
  1216.4 2.1 copy.172
  (185 shorter events, 7.7 us)
Async XLA Ops:
  7.2 67.7 %all-gather.8.cloned.1.call-start = ((), (), s32[]{:S(2)}) async-start(), calls=%async_computation.3 | async-start | bytes 3784704 | tf_op jit(solution)/shard_map/all_gather | solution.py:133
  11.5 144.4 %all-gather.12.cloned.1.call-start = ((), (), s32[]{:S(2)}) async-start(), calls=%async_computation.5 | async-start | bytes 8988672 | tf_op jit(solution)/shard_map/all_gather | solution.py:139
  13.4 12.7 %copy-start.39 = (f32[576]{0:T(1024)S(1)}, f32[576]{0:T(1024)}, u32[]{:S(2)}) copy-start(f32[576]{0:T(1024)} %param.29) | copy-start | bytes 6916
  13.4 12.7 %copy-start.37 = (f32[896]{0:T(1024)S(1)}, f32[896]{0:T(1024)}, u32[]{:S(2)}) copy-start(f32[896]{0:T(1024)} %param.28) | copy-start | bytes 10756
  13.4 18.6 %copy-start.2 = (bf16[256,896]{1,0:T(8,128)(2,1)S(1)}, bf16[256,896]{1,0:T(8,128)(2,1)}, u32[]{:S(2)}) copy-start(bf16[256,896]{1,0:T(8,128)(2,1)} %param.21) | copy-start | bytes 1376260
  13.4 262.6 %all-gather.10.cloned.1.call-start = ((), (), s32[]{:S(2)}) async-start(), calls=%async_computation.4 | async-start | bytes 17977344 | tf_op jit(solution)/shard_map/all_gather | solution.py:136
  23.8 9.1 copy-start.51
  26.0 435.7 %reduce-scatter.7.cloned.1.call-start = ((), (), s32[]{:S(2)}) async-start(), calls=%async_computation.6 | async-start | bytes 3784704 | tf_op jit(solution)/shard_map/reduce_scatter | solution.py:128
  32.1 45.6 %copy-start.30 = (f32[896]{0:T(1024)}, f32[896]{0:T(1024)S(1)}, u32[]{:S(2)}) copy-start(f32[896]{0:T(1024)S(1)} %get-tuple-element.31) | copy-start | bytes 10756
  32.2 0.6 copy-start.41
  32.8 45.7 %copy-start.20 = (bf16[256,8,2,56]{0,3,2,1:T(8,128)(2,1)}, bf16[256,8,2,56]{0,3,2,1:T(8,128)(2,1)S(1)}, u32[]{:S(2)}) copy-start(bf16[256,8,2,56]{0,3,2,1:T(8,128)(2,1)S(1)} %copy.136) | copy-start | bytes 1376260
  75.9 1.8 copy-start.26
  77.6 1.2 copy-start.12
  79.0 1.9 copy-start.24
  79.4 1.5 copy-start.28
  79.6 1.3 copy-start.18
  80.3 1.8 copy-start
  80.3 1.8 copy-start.32
  80.9 1.3 copy-start.33
  82.2 2.5 copy-start.34
  82.2 3.1 copy-start.13
  82.2 73.7 %copy-start.16 = (bf16[256,896]{1,0:T(8,128)(2,1)S(1)}, bf16[256,896]{1,0:T(8,128)(2,1)}, u32[]{:S(2)}) copy-start(bf16[256,896]{1,0:T(8,128)(2,1)} %param.22) | copy-start | bytes 1376260
  84.7 0.6 copy-start.50
  84.7 0.6 copy-start.35
  85.3 196.3 %copy-start.4 = (bf16[256,8,2,56]{0,3,2,1:T(8,128)(2,1)}, bf16[256,8,2,56]{0,3,2,1:T(8,128)(2,1)S(1)}, u32[]{:S(2)}) copy-start(bf16[256,8,2,56]{0,3,2,1:T(8,128)(2,1)S(1)} %copy.143) | copy-start | bytes 1376260
  276.1 5.5 copy-start.52
  290.6 8.1 copy-start.9
  290.6 8.1 copy-start.7
  311.5 3.1 copy-start.1
  311.5 3.1 copy-start.25
  314.7 3.9 copy-start.22
  315.5 0.9 copy-start.19
  315.5 1.6 copy-start.29
  316.4 1.1 copy-start.14
  317.6 1.0 copy-start.21
  318.5 679.3 %copy-start.15 = (bf16[256,14,64]{0,2,1:T(8,128)(2,1)}, bf16[256,14,64]{0,2,1:T(8,128)(2,1)S(1)}, u32[]{:S(2)}) copy-start(bf16[256,14,64]{0,2,1:T(8,128)(2,1)S(1)} %add_convert_fusion) | copy-start | bytes 1376260
  323.4 1.0 copy-start.17
  323.4 1.0 copy-start.45
  323.4 301.7 %reduce-scatter.11.cloned.1.call-start = ((), (), s32[]{:S(2)}) async-start(), calls=%async_computation.11 | async-start | bytes 8988672
  332.5 1.0 copy-start.5
  332.5 665.3 %reduce-scatter.9.cloned.1.call-start = ((), (), s32[]{:S(2)}) async-start(), calls=%async_computation.8 | async-start | bytes 17977344 | tf_op jit(solution)/shard_map/reduce_scatter | solution.py:128
  333.5 4.3 copy-start.8
  354.1 643.8 %copy-start.23 = (bf16[2,64,256]{2,1,0:T(8,128)(2,1)S(1)}, bf16[2,64,256]{2,1,0:T(8,128)(2,1)}, u32[]{:S(2)}) copy-start(bf16[2,64,256]{2,1,0:T(8,128)(2,1)} %copy-done.22) | copy-start | bytes 196612
  354.1 643.8 %copy-start.27 = (bf16[896,128]{1,0:T(8,128)(2,1)S(1)}, bf16[896,128]{1,0:T(8,128)(2,1)}, u32[]{:S(2)}) copy-start(bf16[896,128]{1,0:T(8,128)(2,1)} %copy-done.26) | copy-start | bytes 688132
  354.1 701.8 %all-gather.14.cloned.1.call-start = ((), (), s32[]{:S(2)}) async-start(), calls=%async_computation.7 | async-start | bytes 1949696 | tf_op jit(solution)/shard_map/all_gather | solution.py:314
  461.7 632.9 %all-gather.18.cloned.1.call-start = ((), (), s32[]{:S(2)}) async-start(), calls=%async_computation.10 | async-start | bytes 4630528 | tf_op jit(solution)/shard_map/all_gather | solution.py:312
  625.2 547.4 %all-gather.16.cloned.1.call-start = ((), (), s32[]{:S(2)}) async-start(), calls=%async_computation.9 | async-start | bytes 9261056 | tf_op jit(solution)/shard_map/all_gather | solution.py:313
  1000.1 3.9 copy-start.31
  1000.1 3.9 copy-start.42
  1000.1 4.2 copy-start.36
  1000.2 45.3 %copy-start.44 = (f32[256]{0:T(256)S(1)}, f32[256]{0:T(256)}, u32[]{:S(2)}) copy-start(f32[256]{0:T(256)} %copy-done.43) | copy-start | bytes 3076
  1000.2 45.3 %copy-start.38 = (f32[896]{0:T(1024)S(1)}, f32[896]{0:T(1024)}, u32[]{:S(2)}) copy-start(f32[896]{0:T(1024)} %param.28) | copy-start | bytes 10756
  1000.2 45.3 %copy-start.46 = (f32[896]{0:T(1024)S(1)}, f32[896]{0:T(1024)}, u32[]{:S(2)}) copy-start(f32[896]{0:T(1024)} %param.34) | copy-start | bytes 10756
  1000.2 45.3 %copy-start.47 = (f32[896]{0:T(1024)S(1)}, f32[896]{0:T(1024)}, u32[]{:S(2)}) copy-start(f32[896]{0:T(1024)} %param.40) | copy-start | bytes 10756
  1000.2 45.9 %copy-start.40 = (f32[576]{0:T(1024)S(1)}, f32[576]{0:T(1024)}, u32[]{:S(2)}) copy-start(f32[576]{0:T(1024)} %param.29) | copy-start | bytes 6916
  1000.2 45.9 %copy-start.48 = (f32[576]{0:T(1024)S(1)}, f32[576]{0:T(1024)}, u32[]{:S(2)}) copy-start(f32[576]{0:T(1024)} %param.35) | copy-start | bytes 6916
  1000.2 45.9 %copy-start.49 = (f32[576]{0:T(1024)S(1)}, f32[576]{0:T(1024)}, u32[]{:S(2)}) copy-start(f32[576]{0:T(1024)} %param.41) | copy-start | bytes 6916
  1047.8 9.0 copy-start.3
  1056.8 5.5 copy-start.6
  1056.8 5.5 slice-start.2
  1056.8 5.5 copy-start.10
  1056.9 5.7 copy-start.11
  1172.5 43.9 %slice-start = ((s8[4358144]{0:T(1024)(128)(4,1)}), s8[4194304]{0:T(1024)(128)(4,1)S(1)}, s32[]{:S(2)}) async-start(s8[4358144]{0:T(1024)(128)(4,1)} %bitcast.107), calls=%async_computation.12 | async-start | bytes 8388608
  1176.6 39.9 %slice-start.1 = ((s8[4358144]{0:T(1024)(128)(4,1)}), s8[163840]{0:T(1024)(128)(4,1)S(1)}, s32[]{:S(2)}) async-start(s8[4358144]{0:T(1024)(128)(4,1)} %bitcast.107), calls=%async_computation.13 | async-start | bytes 327680
  (1 other events, 0.6 us)
Sparse Core Ops, SparseCore 0:
  11.6 63.2 all-gather.7
  78.4 77.4 all-gather.11
  159.3 116.6 all-gather.9
  323.5 138.0 reduce-scatter.6
  464.5 160.5 reduce-scatter.10
  628.0 369.7 reduce-scatter.8
  1000.3 41.7 all-gather.13
  1044.5 50.1 all-gather.17
  1097.0 75.4 all-gather.15
